TPU v7x, 512 devices: a whole 4x4x16 slice. The times are simulated.
512 devices in a mesh: span: 64 (over x, z), head: 8 (over y, core).
Axes of the slice: x: 4, y: 4, z: 16, core: 2. Of those that a mesh axis runs over, the one named last changes fastest.
Arguments:
- queries: bfloat16 [8192, 3072], P(('span', 'head'))
- keys: bfloat16 [8192, 3072], P(('span', 'head'))
- values: bfloat16 [8192, 3072], P(('span', 'head')), may hold values from -6 to 6
- cache_keys: bfloat16 [8192, 3072], P('span', 'head'), may hold values from -18 to 18
- cache_values: bfloat16 [8192, 3072], P('span', 'head'), may hold values from -6 to 6
- levels: int32 [16], replicated, may hold values from 0 to 15
- first_span: int32 [16], replicated, may hold values from 0 to 7, as said below
- level_gate: float32 [16, 3072], P(None, 'head'), may hold values from 0.1 to 1.9
Outputs:
- attended: bfloat16 [8192, 3072], P(('span', 'head'))
Inputs may be any that keep to these rules, and one draw needn't show every extreme that they name: first_span[c] lies between 0 and c // 2.
All inputs are finite; a program needn't handle non-finite values.
Results may differ from a plain program's by a relative error of at most 0.0045.
Values may be sent and summed in bfloat16 or wider, within the bound.
A program may use at most 128 MiB of HBM per device.

v0:
```python
import jax
import jax.numpy as jnp
from jax import lax
from jax.sharding import PartitionSpec as P

HD = 128
CL = 512


def passed_along(block, axis, distance):
    devices = range(lax.axis_size(axis))
    route = [(i - distance, i) for i in devices if i - distance in devices]
    return lax.ppermute(block, axis, route)


def update_state(running, query_heads, key_block, value_block, allowed):
    row_peak, totals, accumulated = running
    scores = jnp.einsum(
        "qhd,khd->qhk", query_heads, key_block, preferred_element_type=jnp.float32
    ) * HD ** (-0.5)
    scores = jnp.where(allowed[:, None, :], scores, -jnp.inf)
    new_peak = jnp.maximum(row_peak, jnp.max(scores, axis=2))
    weights = jnp.exp(scores - new_peak[:, :, None])
    shrink = jnp.exp(row_peak - new_peak)
    new_totals = totals * shrink + jnp.sum(weights, axis=2)
    product = jnp.einsum(
        "qhk,khd->qhd",
        weights.astype(jnp.bfloat16),
        value_block,
        preferred_element_type=jnp.float32,
    )
    return (new_peak, new_totals, accumulated * shrink[:, :, None] + product)


def shards(queries, keys, values, cache_keys, cache_values, levels, first_span, level_gate):
    query_all, key_all, value_all = (
        lax.all_to_all(queries, "head", split_axis=1, concat_axis=0, tiled=True),
        lax.all_to_all(keys, "head", split_axis=1, concat_axis=0, tiled=True),
        lax.all_to_all(values, "head", split_axis=1, concat_axis=0, tiled=True),
    )
    row_count = query_all.shape[0]
    width_dev = query_all.shape[1]
    head_count = width_dev // HD
    span_width = lax.axis_size("span")
    my_index = lax.axis_index("span")
    row_span = my_index * row_count // CL
    row_first = first_span[row_span]
    query_heads = query_all.reshape(row_count, head_count, HD)
    empty_state = (
        jnp.full((row_count, head_count), -jnp.inf, jnp.float32),
        jnp.zeros((row_count, head_count), jnp.float32),
        jnp.zeros((row_count, head_count, HD), jnp.float32),
    )
    all_true = jnp.ones((row_count, row_count), dtype=bool)
    running = update_state(
        empty_state,
        query_heads,
        key_all.reshape(row_count, head_count, HD),
        value_all.reshape(row_count, head_count, HD),
        all_true,
    )
    group_size = CL // row_count
    offsets = []
    for step in range(1, group_size):
        offsets.append(step)
        offsets.append(-step)
    for by_step in offsets:
        moved = passed_along((key_all, value_all), "span", by_step)
        source = my_index - by_step
        valid = (source >= 0) & (source < span_width) & (source * row_count // CL == row_span)
        running = update_state(
            running,
            query_heads,
            moved[0].reshape(row_count, head_count, HD),
            moved[1].reshape(row_count, head_count, HD),
            all_true & valid,
        )
    key_piece = lax.all_gather(cache_keys, "span", axis=0, tiled=True)
    value_piece = lax.all_gather(cache_values, "span", axis=0, tiled=True)
    length = key_piece.shape[0]
    piece_span = jnp.arange(length, dtype=jnp.int32) // CL
    visible = (piece_span >= row_first) & (piece_span < row_span)
    allowed = jnp.broadcast_to(visible[None, :], (row_count, length))
    running = update_state(
        running,
        query_heads,
        key_piece.reshape(length, head_count, HD),
        value_piece.reshape(length, head_count, HD),
        allowed,
    )
    row_peak, totals, accumulated = running
    level_count = level_gate.shape[0]
    one_hot = (levels[row_span] == jnp.arange(level_count, dtype=jnp.int32)).astype(jnp.float32)
    gates = jnp.dot(one_hot[None, :], level_gate, precision=lax.Precision.HIGHEST)
    gate_rows = gates.reshape(1, head_count, HD)
    result = accumulated / totals[:, :, None] * gate_rows
    result = result.reshape(row_count, width_dev).astype(jnp.bfloat16)
    return lax.all_to_all(result, "head", split_axis=0, concat_axis=1, tiled=True)


def solution(mesh):
    placed = (
        P(("span", "head"), None),
        P(("span", "head"), None),
        P(("span", "head"), None),
        P("span", "head"),
        P("span", "head"),
        P(),
        P(),
        P(None, "head"),
    )
    return jax.shard_map(
        shards, mesh=mesh, in_specs=placed, out_specs=P(("span", "head"), None), check_vma=False
    )
```

profile of v0, /device:TPU:1, one launch (start us, length us, event | category | flops | bytes accessed | tf_op | source)
XLA Modules:
  0.0 364.1 jit_solution(17938896526394091521)
XLA Ops:
  6.5 1.6 copy.161
  8.2 1.6 copy.164
  9.9 1.5 copy.214
  11.4 10.1 %all-to-all-start = ((bf16[16,8,384]{2,0,1:T(8,128)(2,1)}), bf16[16,8,384]{2,0,1:T(8,128)(2,1)S(1)}, u32[]{:S(2)}, u32[]{:S(2)}) async-start(bf16[16,8,384]{2,0,1:T(8,128)(2,1)} %bitcast.150), calls=%async_computation | async-start | bytes 196608 | tf_op jit(solution)/shard_map/all_to_all | solution.py:38
  21.6 1.5 copy.213
  24.4 2.2 all-to-all-done
  26.6 4.1 %all-to-all-start.1 = ((bf16[16,8,384]{2,0,1:T(8,128)(2,1)}), bf16[16,8,384]{2,0,1:T(8,128)(2,1)S(1)}, u32[]{:S(2)}, u32[]{:S(2)}) async-start(bf16[16,8,384]{2,0,1:T(8,128)(2,1)} %bitcast.149), calls=%async_computation.1 | async-start | bytes 196608 | tf_op jit(solution)/shard_map/all_to_all | solution.py:37
  32.6 1.5 copy.212
  35.5 5.8 %collective-permute-start.8 = (bf16[128,384]{1,0:T(8,128)(2,1)S(1)}, bf16[128,384]{1,0:T(8,128)(2,1)S(1)}, u32[]{:S(2)}, u32[]{:S(2)}) collective-permute-start(bf16[128,384]{1,0:T(8,128)(2,1)S(1)} %bitcast.155), channel_id=1, source_target_pairs={{0,24},{8,32},{16,40},{24,48},{32,56},{40,64},{48,72},{56,80},{64,... | collective-permute-start | bytes 294920 | tf_op jit(solution)/shard_map/ppermute | solution.py:13
  41.3 5.4 %all-to-all-start.2 = ((bf16[16,8,384]{2,0,1:T(8,128)(2,1)}), bf16[16,8,384]{2,0,1:T(8,128)(2,1)S(1)}, u32[]{:S(2)}, u32[]{:S(2)}) async-start(bf16[16,8,384]{2,0,1:T(8,128)(2,1)} %bitcast.148), calls=%async_computation.2 | async-start | bytes 196608 | tf_op jit(solution)/shard_map/all_to_all | solution.py:39
  48.5 4.9 %collective-permute-start.4 = (bf16[128,384]{1,0:T(8,128)(2,1)S(1)}, bf16[128,384]{1,0:T(8,128)(2,1)S(1)}, u32[]{:S(2)}, u32[]{:S(2)}) collective-permute-start(bf16[128,384]{1,0:T(8,128)(2,1)S(1)} %bitcast.157), channel_id=1, source_target_pairs={{0,16},{8,24},{16,32},{24,40},{32,48},{40,56},{48,64},{56,72},{64,... | collective-permute-start | bytes 294920 | tf_op jit(solution)/shard_map/ppermute | solution.py:13
  54.9 4.0 %collective-permute-start = (bf16[128,384]{1,0:T(8,128)(2,1)S(1)}, bf16[128,384]{1,0:T(8,128)(2,1)S(1)}, u32[]{:S(2)}, u32[]{:S(2)}) collective-permute-start(bf16[128,384]{1,0:T(8,128)(2,1)S(1)} %bitcast.160), channel_id=1, source_target_pairs={{0,8},{8,16},{16,24},{24,32},{32,40},{40,48},{48,56},{56,64},{64,7... | collective-permute-start | bytes 294920 | tf_op jit(solution)/shard_map/ppermute | solution.py:13
  58.9 2.8 collective-permute-start.1
  63.2 7.2 %collective-permute-start.5 = (bf16[128,384]{1,0:T(8,128)(2,1)S(1)}, bf16[128,384]{1,0:T(8,128)(2,1)S(1)}, u32[]{:S(2)}, u32[]{:S(2)}) collective-permute-start(bf16[128,384]{1,0:T(8,128)(2,1)S(1)} %bitcast.165), channel_id=1, source_target_pairs={{0,16},{8,24},{16,32},{24,40},{32,48},{40,56},{48,64},{56,72},{64,... | collective-permute-start | bytes 294920 | tf_op jit(solution)/shard_map/ppermute | solution.py:13
  71.8 6.1 %collective-permute-start.9 = (bf16[128,384]{1,0:T(8,128)(2,1)S(1)}, bf16[128,384]{1,0:T(8,128)(2,1)S(1)}, u32[]{:S(2)}, u32[]{:S(2)}) collective-permute-start(bf16[128,384]{1,0:T(8,128)(2,1)S(1)} %bitcast.167), channel_id=1, source_target_pairs={{0,24},{8,32},{16,40},{24,48},{32,56},{40,64},{48,72},{56,80},{64,... | collective-permute-start | bytes 294920 | tf_op jit(solution)/shard_map/ppermute | solution.py:13
  80.5 1.7 collective-permute-done.9
  82.4 3.9 %collective-permute-done.11 = bf16[128,384]{1,0:T(8,128)(2,1)S(1)} collective-permute-done((bf16[128,384]{1,0:T(8,128)(2,1)S(1)}, bf16[128,384]{1,0:T(8,128)(2,1)S(1)}, u32[]{:S(2)}, u32[]{:S(2)}) %collective-permute-start.11) | collective-permute-done | bytes 98336 | tf_op jit(solution)/shard_map/ppermute | solution.py:13
  87.9 85.2 %all-gather.3.cloned.1.call-done = bf16[8192,384]{0,1:T(8,128)(2,1)} async-done(((bf16[128,384]{0,1:T(8,128)(2,1)}), bf16[8192,384]{0,1:T(8,128)(2,1)}) %all-gather.3.cloned.1.call-update) | async-done | bytes 6291472 | tf_op jit(solution)/shard_map/all_gather | solution.py:78
  173.2 7.7 %bitcast_reduce_fusion = (f32[128,3]{0,1:T(4,128)S(1)}, f32[3,8192,128]{2,1,0:T(8,128)S(1)}) fusion(bf16[8192,3,128]{0,2,1:T(8,128)(2,1)} %bitcast.153, bf16[128,3,128]{2,0,1:T(8,128)(2,1)S(1)} %copy.121, pred[8192]{0:T(1024)(128)(4,1)S(1)} %fusion.74), kind=kOutput, calls=%fused_computation.1 | convolution fusion | flops 814743168 | bytes 18982400 | tf_op jit(solution)/shard_map/qhd,khd->qhk/dot_general | solution.py:18
  180.9 4.5 %copy-done.1 = f32[3,8192,128]{2,1,0:T(8,128)} copy-done((f32[3,8192,128]{2,1,0:T(8,128)}, f32[3,8192,128]{2,1,0:T(8,128)S(1)}, u32[]{:S(2)}) %copy-start.1) | copy-done | bytes 12582936
  185.5 1.7 fusion.1
  187.1 140.4 %all-gather.5.cloned.1.call-done = bf16[8192,384]{0,1:T(8,128)(2,1)} async-done(((bf16[128,384]{0,1:T(8,128)(2,1)}), bf16[8192,384]{0,1:T(8,128)(2,1)}) %all-gather.5.cloned.1.call-update) | async-done | bytes 6291472 | tf_op jit(solution)/shard_map/all_gather | solution.py:79
  327.6 9.2 %fusion.36 = f32[128,3,128]{2,0,1:T(8,128)S(1)} fusion(bf16[8192,3,128]{0,2,1:T(8,128)(2,1)} %bitcast.152, f32[3,8192,128]{2,1,0:T(8,128)} %copy-done.1, f32[128,3]{0,1:T(4,128)S(1)} %get-tuple-element.13), kind=kOutput, calls=%fused_computation.52 | convolution fusion | flops 811597824 | bytes 19072512 | tf_op jit(solution)/shard_map/qhk,khd->qhd/dot_general | solution.py:26
  338.9 17.7 %all_to_all.70 = bf16[8,16,384]{2,1,0:T(8,128)(2,1)S(1)} all-to-all(bf16[8,16,384]{2,1,0:T(8,128)(2,1)S(1)} %convert_element_type.41), channel_id=1, replica_groups=mesh['span'=64,'head'=8] {'head'}, dimensions={0} | all-to-all | bytes 196608 | tf_op jit(solution)/shard_map/all_to_all | solution.py:98
  (69 shorter events, 17.9 us)
Async XLA Ops:
  6.5 24.1 %copy-start = (f32[16,384]{1,0:T(8,128)S(1)}, f32[16,384]{1,0:T(8,128)}, u32[]{:S(2)}) copy-start(f32[16,384]{1,0:T(8,128)} %param.15) | copy-start | bytes 73732
  6.5 166.6 %all-gather.3.cloned.1.call-start = ((), (), s32[]{:S(2)}) async-start(), calls=%async_computation.4 | async-start | bytes 6389760 | tf_op jit(solution)/shard_map/all_gather | solution.py:78
  8.2 319.4 %all-gather.5.cloned.1.call-start = ((), (), s32[]{:S(2)}) async-start(), calls=%async_computation.5 | async-start | bytes 6389760 | tf_op jit(solution)/shard_map/all_gather | solution.py:79
  11.4 15.1 %all-to-all-start = ((bf16[16,8,384]{2,0,1:T(8,128)(2,1)}), bf16[16,8,384]{2,0,1:T(8,128)(2,1)S(1)}, u32[]{:S(2)}, u32[]{:S(2)}) async-start(bf16[16,8,384]{2,0,1:T(8,128)(2,1)} %bitcast.150), calls=%async_computation | async-start | bytes 196608 | tf_op jit(solution)/shard_map/all_to_all | solution.py:38
  26.6 14.7 %all-to-all-start.1 = ((bf16[16,8,384]{2,0,1:T(8,128)(2,1)}), bf16[16,8,384]{2,0,1:T(8,128)(2,1)S(1)}, u32[]{:S(2)}, u32[]{:S(2)}) async-start(bf16[16,8,384]{2,0,1:T(8,128)(2,1)} %bitcast.149), calls=%async_computation.1 | async-start | bytes 196608 | tf_op jit(solution)/shard_map/all_to_all | solution.py:37
  34.2 20.7 %collective-permute-start.10 = (bf16[128,384]{1,0:T(8,128)(2,1)S(1)}, bf16[128,384]{1,0:T(8,128)(2,1)S(1)}, u32[]{:S(2)}, u32[]{:S(2)}) collective-permute-start(bf16[128,384]{1,0:T(8,128)(2,1)S(1)} %bitcast.154), channel_id=1, source_target_pairs={{24,0},{32,8},{40,16},{48,24},{56,32},{64,40},{72,48},{80,56},{88,... | collective-permute-start | bytes 294920 | tf_op jit(solution)/shard_map/ppermute | solution.py:13
  35.5 23.4 %collective-permute-start.8 = (bf16[128,384]{1,0:T(8,128)(2,1)S(1)}, bf16[128,384]{1,0:T(8,128)(2,1)S(1)}, u32[]{:S(2)}, u32[]{:S(2)}) collective-permute-start(bf16[128,384]{1,0:T(8,128)(2,1)S(1)} %bitcast.155), channel_id=1, source_target_pairs={{0,24},{8,32},{16,40},{24,48},{32,56},{40,64},{48,72},{56,80},{64,... | collective-permute-start | bytes 294920 | tf_op jit(solution)/shard_map/ppermute | solution.py:13
  41.3 17.6 %all-to-all-start.2 = ((bf16[16,8,384]{2,0,1:T(8,128)(2,1)}), bf16[16,8,384]{2,0,1:T(8,128)(2,1)S(1)}, u32[]{:S(2)}, u32[]{:S(2)}) async-start(bf16[16,8,384]{2,0,1:T(8,128)(2,1)} %bitcast.148), calls=%async_computation.2 | async-start | bytes 196608 | tf_op jit(solution)/shard_map/all_to_all | solution.py:39
  47.2 14.7 %collective-permute-start.6 = (bf16[128,384]{1,0:T(8,128)(2,1)S(1)}, bf16[128,384]{1,0:T(8,128)(2,1)S(1)}, u32[]{:S(2)}, u32[]{:S(2)}) collective-permute-start(bf16[128,384]{1,0:T(8,128)(2,1)S(1)} %bitcast.156), channel_id=1, source_target_pairs={{16,0},{24,8},{32,16},{40,24},{48,32},{56,40},{64,48},{72,56},{80,... | collective-permute-start | bytes 294920 | tf_op jit(solution)/shard_map/ppermute | solution.py:13
  48.5 14.7 %collective-permute-start.4 = (bf16[128,384]{1,0:T(8,128)(2,1)S(1)}, bf16[128,384]{1,0:T(8,128)(2,1)S(1)}, u32[]{:S(2)}, u32[]{:S(2)}) collective-permute-start(bf16[128,384]{1,0:T(8,128)(2,1)S(1)} %bitcast.157), channel_id=1, source_target_pairs={{0,16},{8,24},{16,32},{24,40},{32,48},{40,56},{48,64},{56,72},{64,... | collective-permute-start | bytes 294920 | tf_op jit(solution)/shard_map/ppermute | solution.py:13
  53.4 17.0 %collective-permute-start.2 = (bf16[128,384]{1,0:T(8,128)(2,1)S(1)}, bf16[128,384]{1,0:T(8,128)(2,1)S(1)}, u32[]{:S(2)}, u32[]{:S(2)}) collective-permute-start(bf16[128,384]{1,0:T(8,128)(2,1)S(1)} %bitcast.158), channel_id=1, source_target_pairs={{8,0},{16,8},{24,16},{32,24},{40,32},{48,40},{56,48},{64,56},{72,6... | collective-permute-start | bytes 294920 | tf_op jit(solution)/shard_map/ppermute | solution.py:13
  54.9 16.9 %collective-permute-start = (bf16[128,384]{1,0:T(8,128)(2,1)S(1)}, bf16[128,384]{1,0:T(8,128)(2,1)S(1)}, u32[]{:S(2)}, u32[]{:S(2)}) collective-permute-start(bf16[128,384]{1,0:T(8,128)(2,1)S(1)} %bitcast.160), channel_id=1, source_target_pairs={{0,8},{8,16},{16,24},{24,32},{32,40},{40,48},{48,56},{56,64},{64,7... | collective-permute-start | bytes 294920 | tf_op jit(solution)/shard_map/ppermute | solution.py:13
  58.9 19.0 %collective-permute-start.1 = (bf16[128,384]{1,0:T(8,128)(2,1)S(1)}, bf16[128,384]{1,0:T(8,128)(2,1)S(1)}, u32[]{:S(2)}, u32[]{:S(2)}) collective-permute-start(bf16[128,384]{1,0:T(8,128)(2,1)S(1)} %bitcast.162), channel_id=1, source_target_pairs={{0,8},{8,16},{16,24},{24,32},{32,40},{40,48},{48,56},{56,64},{64,7... | collective-permute-start | bytes 294920 | tf_op jit(solution)/shard_map/ppermute | solution.py:13
  61.9 18.2 %collective-permute-start.3 = (bf16[128,384]{1,0:T(8,128)(2,1)S(1)}, bf16[128,384]{1,0:T(8,128)(2,1)S(1)}, u32[]{:S(2)}, u32[]{:S(2)}) collective-permute-start(bf16[128,384]{1,0:T(8,128)(2,1)S(1)} %bitcast.164), channel_id=1, source_target_pairs={{8,0},{16,8},{24,16},{32,24},{40,32},{48,40},{56,48},{64,56},{72,6... | collective-permute-start | bytes 294920 | tf_op jit(solution)/shard_map/ppermute | solution.py:13
  63.2 17.0 %collective-permute-start.5 = (bf16[128,384]{1,0:T(8,128)(2,1)S(1)}, bf16[128,384]{1,0:T(8,128)(2,1)S(1)}, u32[]{:S(2)}, u32[]{:S(2)}) collective-permute-start(bf16[128,384]{1,0:T(8,128)(2,1)S(1)} %bitcast.165), channel_id=1, source_target_pairs={{0,16},{8,24},{16,32},{24,40},{32,48},{40,56},{48,64},{56,72},{64,... | collective-permute-start | bytes 294920 | tf_op jit(solution)/shard_map/ppermute | solution.py:13
  70.4 9.9 %collective-permute-start.7 = (bf16[128,384]{1,0:T(8,128)(2,1)S(1)}, bf16[128,384]{1,0:T(8,128)(2,1)S(1)}, u32[]{:S(2)}, u32[]{:S(2)}) collective-permute-start(bf16[128,384]{1,0:T(8,128)(2,1)S(1)} %bitcast.166), channel_id=1, source_target_pairs={{16,0},{24,8},{32,16},{40,24},{48,32},{56,40},{64,48},{72,56},{80,... | collective-permute-start | bytes 294920 | tf_op jit(solution)/shard_map/ppermute | solution.py:13
  71.8 10.5 %collective-permute-start.9 = (bf16[128,384]{1,0:T(8,128)(2,1)S(1)}, bf16[128,384]{1,0:T(8,128)(2,1)S(1)}, u32[]{:S(2)}, u32[]{:S(2)}) collective-permute-start(bf16[128,384]{1,0:T(8,128)(2,1)S(1)} %bitcast.167), channel_id=1, source_target_pairs={{0,24},{8,32},{16,40},{24,48},{32,56},{40,64},{48,72},{56,80},{64,... | collective-permute-start | bytes 294920 | tf_op jit(solution)/shard_map/ppermute | solution.py:13
  77.8 8.4 %collective-permute-start.11 = (bf16[128,384]{1,0:T(8,128)(2,1)S(1)}, bf16[128,384]{1,0:T(8,128)(2,1)S(1)}, u32[]{:S(2)}, u32[]{:S(2)}) collective-permute-start(bf16[128,384]{1,0:T(8,128)(2,1)S(1)} %bitcast.168), channel_id=1, source_target_pairs={{24,0},{32,8},{40,16},{48,24},{56,32},{64,40},{72,48},{80,56},{88,... | collective-permute-start | bytes 294920 | tf_op jit(solution)/shard_map/ppermute | solution.py:13
  180.9 4.6 %copy-start.1 = (f32[3,8192,128]{2,1,0:T(8,128)}, f32[3,8192,128]{2,1,0:T(8,128)S(1)}, u32[]{:S(2)}) copy-start(f32[3,8192,128]{2,1,0:T(8,128)S(1)} %get-tuple-element.22) | copy-start | bytes 37748740
Sparse Core Ops, SparseCore 0:
  10.3 162.8 all-gather.2
  176.1 151.4 all-gather.4
where the time goes:
time: 365 us; the launch traced here: 364 us
  waiting for transfers between devices  234 us (64%)
  starting transfers between devices  58.1 us (16%)
  matrix products  21 us (6%)
  blocking collectives  17.7 us (5%)
  local copies, waits for them, and re-layouts  17.4 us (5%)
  between operations  13.8 us (4%)
    all_gather x1, waiting for transfers between devices, shards(): value_piece = lax.all_gather(cache_values, 'span', axis=0, tiled=True)  140 us
    all_gather x1, waiting for transfers between devices, shards(): key_piece = lax.all_gather(cache_keys, 'span', axis=0, tiled=True)  85.2 us
    ppermute x12, starting transfers between devices, passed_along(): return lax.ppermute(block, axis, route)  38.5 us
    all_to_all x1, blocking collectives, shards(): lax.all_to_all(result, 'head', split_axis=0, concat_axis=1, tiled=True)  17.7 us
    dot_general x8, matrix products, update_state(): jnp.einsum('qhk,khd->qhd', weights.astype(jnp.bfloat16), value_block, pre...  10.8 us
    all_to_all x1, starting transfers between devices, shards(): lax.all_to_all(keys, 'head', split_axis=1, concat_axis=0, tiled=True)  10.1 us
    dot_general x8, matrix products, update_state(): jnp.einsum('qhd,khd->qhk', query_heads, key_block, preferred_element_type...  9.5 us
    unnamed x6, local copies, waits for them, and re-layouts  7.82 us
  transfers between devices with their start and end apart: 17, of which 5 were waited for; matrix products, arithmetic and copies ran while one was open for 6% of the time, Pallas kernels for 0%

commit v1 on v0

v1 whole, which is shorter than its diff:
```python
import functools
import math

import jax
import jax.numpy as jnp
from jax import lax
from jax.experimental import pallas as pl
from jax.experimental.pallas import tpu as pltpu
from jax.sharding import PartitionSpec as P

HD = 128
CL = 512
NX, NZ, NH = 4, 16, 8
NR = 4
J = 3
ROWS = 128
WIDTH = J * HD
TOK = 16
QS = NX * ROWS
LOW = -3.0e38
SCALE = HD**-0.5 * math.log2(math.e)
BF = jnp.bfloat16
F32 = jnp.float32
MESH = pl.DeviceIdType.MESH


def kernel(
    q_in, k_in, v_in, ck_in, cv_in, levels, first, gate_in, out,
    kb, vt, cvv, gate, q_all, k_all, v_all, qx, qt, acc, m_st, l_st,
    cq, ck2, cv2, o_send, s_send, o_cur, s_cur, p_send, ps_send, p_rec, ps_rec, o_fin,
    ring_s, ring_r, y_s, y_r, x_s, x_r, c_s, c_r, oc_s, oc_r, p_s, p_r, out_s, out_r, loc,
):
    s = lax.axis_index("span")
    h = lax.axis_index("head")
    x = s // NZ
    z = s % NZ
    zq = z // NR
    r = z % NR
    core = h % 2

    def at(xx, zz):
        return xx * NZ + zz

    right = at(x, (z + 1) % NZ)
    left = at(x, (z + NZ - 1) % NZ)

    def remote(src, dst, send, recv, span, head):
        return pltpu.make_async_remote_copy(
            src_ref=src, dst_ref=dst, send_sem=send, recv_sem=recv,
            device_id=(span, head), device_id_type=MESH,
        )

    cp_v = pltpu.make_async_copy(cv_in, cvv, loc.at[0])
    cp_k = pltpu.make_async_copy(ck_in, kb.at[0], loc.at[1])
    cp_g = pltpu.make_async_copy(gate_in, gate, loc.at[2])
    cp_v.start()
    cp_k.start()
    cp_g.start()

    barrier = pltpu.get_barrier_semaphore()
    for o in range(1, NH):
        pl.semaphore_signal(barrier, inc=1, device_id=(s, (h + o) % NH), device_id_type=MESH)
    for o in range(1, NX):
        pl.semaphore_signal(barrier, inc=1, device_id=(at((x + o) % NX, z), h), device_id_type=MESH)
    for o in range(1, NR):
        pl.semaphore_signal(
            barrier, inc=1, device_id=(at(x, zq * NR + (r + o) % NR), h), device_id_type=MESH
        )
    for n in (right, left):
        pl.semaphore_signal(barrier, inc=1, device_id=(n, h), device_id_type=MESH)

    p_rec[...] = jnp.zeros_like(p_rec)
    row8 = lax.broadcasted_iota(jnp.int32, (8, ROWS), 0)
    empty = jnp.where(row8 < J, LOW, 0.0).astype(F32)
    for i in range(NX):
        ps_rec[i] = empty
    acc[...] = jnp.zeros_like(acc)
    m_st[...] = jnp.full_like(m_st, LOW)
    l_st[...] = jnp.zeros_like(l_st)
    cp_v.wait()
    for j in range(J):
        vt[0, j * HD : (j + 1) * HD, :] = cvv[:, j * HD : (j + 1) * HD].T
    cp_k.wait()
    cp_g.wait()

    pl.semaphore_wait(barrier, NH - 1 + NX - 1 + NR - 1 + 2)

    def ring(d, kv, t):
        buf = kb if kv == 0 else vt
        if d == 0:
            return remote(buf.at[t - 1], buf.at[t], ring_s.at[d, kv, t], ring_r.at[d, kv, t], right, h)
        src = (NZ + 1 - t) % NZ if isinstance(t, int) else NZ + 1 - t
        return remote(buf.at[src], buf.at[NZ - t], ring_s.at[d, kv, t], ring_r.at[d, kv, t], left, h)

    for kv in (0, 1):
        for d in (0, 1):
            ring(d, kv, 1).start()

    fresh = ((q_in, q_all), (k_in, k_all), (v_in, v_all))

    def to_heads(i, o):
        src, dst = fresh[i]
        n = (h + o) % NH
        return remote(
            src.at[:, pl.ds(pl.multiple_of(n * WIDTH, HD), WIDTH)],
            dst.at[pl.ds(pl.multiple_of(h * TOK, TOK), TOK), :],
            y_s.at[i, o], y_r.at[i, o], s, n,
        )

    def own_heads(i):
        src, dst = fresh[i]
        return pltpu.make_async_copy(
            src.at[:, pl.ds(pl.multiple_of(h * WIDTH, HD), WIDTH)],
            dst.at[pl.ds(pl.multiple_of(h * TOK, TOK), TOK), :],
            loc.at[i],
        )

    for i in range(3):
        own_heads(i).start()
        for o in range(1, NH):
            to_heads(i, o).start()

    def heads_arrived(i):
        own_heads(i).wait()
        for o in range(1, NH):
            to_heads(i, o).wait_recv()

    def to_row(o):
        return remote(q_all, qx.at[x], x_s.at[o], x_r.at[o], at((x + o) % NX, z), h)

    heads_arrived(0)
    for o in range(1, NX):
        to_row(o).start()
    own_q = pltpu.make_async_copy(q_all, qx.at[x], loc.at[0])
    own_q.start()

    mine = r - core
    takes = (mine >= 0) & (mine < J)

    def to_taker(i, o):
        n = (r + o) % NR
        j = jnp.clip(n - core, 0, J - 1)
        src = (q_all, k_all, v_all)[i].at[:, pl.ds(pl.multiple_of(j * HD, HD), HD)]
        dst = (cq, ck2, cv2)[i].at[r]
        return remote(src, dst, c_s.at[i, o], c_r.at[i, o], at(x, zq * NR + n), h)

    def own_taken(i):
        j = jnp.clip(mine, 0, J - 1)
        src = (q_all, k_all, v_all)[i].at[:, pl.ds(pl.multiple_of(j * HD, HD), HD)]
        return pltpu.make_async_copy(src, (cq, ck2, cv2)[i].at[r], loc.at[3 + i])

    def sends_to(o):
        n = (r + o) % NR
        return (n - core >= 0) & (n - core < J)

    heads_arrived(1)
    heads_arrived(2)
    for o in range(1, NR):

        @pl.when(sends_to(o))
        def _():
            for i in range(3):
                to_taker(i, o).start()

    @pl.when(takes)
    def _():
        for i in range(3):
            own_taken(i).start()

    def forward(t):
        for kv in (0, 1):
            for d in (0, 1):
                ring(d, kv, t).wait_recv()
                ring(d, kv, t + 1).start()

    forward(1)

    own_q.wait()
    for o in range(1, NX):
        to_row(o).wait_recv()
    for i in range(NX):
        for j in range(J):
            qt[j, :, i * ROWS : (i + 1) * ROWS] = qx[i, :, j * HD : (j + 1) * HD].T

    lane_row = lax.broadcasted_iota(jnp.int32, (1, QS), 1) // ROWS
    q_span = lane_row * NR + zq
    q_first = jnp.zeros((1, QS), jnp.int32)
    for i in range(NX):
        q_first = jnp.where(lane_row == i, first[i * NR + zq], q_first)

    def sees(slot):
        c = x * NR + ((z - slot + NZ) % NZ) // NR
        return (q_first <= c) & (q_span > c)

    def attend(a, b):
        see_a, see_b = sees(a), sees(b)
        for j in range(J):
            cols = slice(j * HD, (j + 1) * HD)
            query = qt[j]
            sa = jnp.dot(kb[a, :, cols], query, preferred_element_type=F32)
            sb = jnp.dot(kb[b, :, cols], query, preferred_element_type=F32)
            ma = jnp.where(see_a, jnp.max(sa, axis=0, keepdims=True) * SCALE, LOW)
            mb = jnp.where(see_b, jnp.max(sb, axis=0, keepdims=True) * SCALE, LOW)
            old = m_st[j]
            peak = jnp.maximum(old, jnp.maximum(ma, mb))
            pa = jnp.exp2(sa * SCALE - jnp.where(see_a, peak, jnp.inf))
            pb = jnp.exp2(sb * SCALE - jnp.where(see_b, peak, jnp.inf))
            shrink = jnp.exp2(old - peak)
            m_st[j] = peak
            l_st[j] = (
                l_st[j] * shrink
                + jnp.sum(pa, axis=0, keepdims=True)
                + jnp.sum(pb, axis=0, keepdims=True)
            )
            product = jnp.dot(vt[a, cols, :], pa.astype(BF), preferred_element_type=F32)
            product += jnp.dot(vt[b, cols, :], pb.astype(BF), preferred_element_type=F32)
            acc[j] = acc[j] * shrink + product

    def step(t, carry):
        attend(t, NZ - t)
        forward(t + 1)
        return carry

    lax.fori_loop(1, 3, step, 0)

    def to_rows_of_span(i, o):
        n = (r + o) % NR
        j = jnp.clip(mine, 0, J - 1)
        src = (o_send, s_send)[i].at[n]
        dst = (o_cur, s_cur)[i].at[j]
        return remote(src, dst, oc_s.at[i, o], oc_r.at[i, o], at(x, zq * NR + n), h)

    def own_part(i):
        j = jnp.clip(mine, 0, J - 1)
        return pltpu.make_async_copy((o_send, s_send)[i].at[r], (o_cur, s_cur)[i].at[j], loc.at[3 + i])

    @pl.when(takes)
    def _():
        for i in range(3):
            own_taken(i).wait()
            for o in range(1, NR):
                to_taker(i, o).wait_recv()
        query = jnp.concatenate([cq[i].T for i in range(NR)], axis=1)
        keys = ck2[...].reshape(CL, HD)
        value = jnp.concatenate([cv2[i].T for i in range(NR)], axis=1)
        scores = jnp.dot(keys, query, preferred_element_type=F32)
        peak = jnp.max(scores, axis=0, keepdims=True) * SCALE
        weights = jnp.exp2(scores * SCALE - peak)
        total = jnp.sum(weights, axis=0, keepdims=True)
        part = jnp.dot(value, weights.astype(BF), preferred_element_type=F32) / total
        for i in range(NR):
            lanes = slice(i * ROWS, (i + 1) * ROWS)
            o_send[i] = part[:, lanes].astype(BF)
            s_send[i] = jnp.where(row8 == 0, peak[:, lanes], total[:, lanes])
        for i in range(2):
            own_part(i).start()
            for o in range(1, NR):
                to_rows_of_span(i, o).start()

    lax.fori_loop(3, 6, step, 0)

    attend(6, NZ - 6)
    for kv in (0, 1):
        for d in (0, 1):
            ring(d, kv, 7).wait_recv()
        ring(kv, kv, 8).start()
    attend(7, NZ - 7)
    for kv in (0, 1):
        ring(kv, kv, 8).wait_recv()
    attend(0, 8)

    def to_owner(i, o):
        n = (x + o) % NX
        src = (p_send, ps_send)[i].at[n]
        dst = (p_rec, ps_rec)[i].at[x]
        return remote(src, dst, p_s.at[i, o], p_r.at[i, o], at(n, z), h)

    for i in range(NX):
        lanes = slice(i * ROWS, (i + 1) * ROWS)
        stats = empty
        for j in range(J):
            total = l_st[j][:, lanes]
            p_send[i, j * HD : (j + 1) * HD, :] = (
                acc[j][:, lanes] / jnp.where(total > 0.0, total, 1.0)
            ).astype(BF)
            stats = jnp.where(row8 == j, m_st[j][:, lanes], stats)
            stats = jnp.where(row8 == J + j, total, stats)
        ps_send[i] = stats
    for o in range(1, NX):

        @pl.when(x + o < NX)
        def _():
            for i in range(2):
                to_owner(i, o).start()

    @pl.when(takes)
    def _():
        for i in range(2):
            own_part(i).wait()

    for o in range(1, NR):
        n = (r - o + NR) % NR

        @pl.when((n - core >= 0) & (n - core < J))
        def _():
            for i in range(2):
                remote(
                    (o_send, s_send)[i].at[0], (o_cur, s_cur)[i].at[jnp.clip(n - core, 0, J - 1)],
                    oc_s.at[i, o], oc_r.at[i, o], at(x, zq * NR + n), h,
                ).wait_recv()

    p_rec[x] = p_send[x]
    ps_rec[x] = ps_send[x]
    for o in range(1, NX):

        @pl.when(x - o >= 0)
        def _():
            for i in range(2):
                to_owner(i, o).wait_recv()

    level = levels[x * NR + zq]
    level_row = lax.broadcasted_iota(jnp.int32, (16, WIDTH), 0)
    gate_row = jnp.sum(jnp.where(level_row == level, gate[...], 0.0), axis=0, keepdims=True)
    for j in range(J):
        cols = slice(j * HD, (j + 1) * HD)
        stat = s_cur[j]
        peaks = [stat[0:1]] + [ps_rec[i][j : j + 1] for i in range(NX)]
        totals = [stat[1:2]] + [ps_rec[i][J + j : J + j + 1] for i in range(NX)]
        parts = [o_cur[j]] + [p_rec[i, cols, :] for i in range(NX)]
        peak = functools.reduce(jnp.maximum, peaks)
        shares = [t * jnp.exp2(p - peak) for t, p in zip(totals, peaks)]
        whole = functools.reduce(jnp.add, shares)
        mixed = functools.reduce(jnp.add, [w * p.astype(F32) for w, p in zip(shares, parts)]) / whole
        o_fin[:, cols] = (mixed.T * gate_row[:, cols]).astype(BF)

    def to_tokens(o):
        n = (h + o) % NH
        return remote(
            o_fin.at[pl.ds(pl.multiple_of(n * TOK, TOK), TOK), :],
            out.at[:, pl.ds(pl.multiple_of(h * WIDTH, HD), WIDTH)],
            out_s.at[o], out_r.at[o], s, n,
        )

    own_out = pltpu.make_async_copy(
        o_fin.at[pl.ds(pl.multiple_of(h * TOK, TOK), TOK), :],
        out.at[:, pl.ds(pl.multiple_of(h * WIDTH, HD), WIDTH)],
        loc.at[0],
    )
    for o in range(1, NH):
        to_tokens(o).start()
    own_out.start()

    for kv in (0, 1):
        for d in (0, 1):
            for t in range(1, 8):
                ring(d, kv, t).wait_send()
        ring(kv, kv, 8).wait_send()
    for i in range(3):
        for o in range(1, NH):
            to_heads(i, o).wait_send()
    for o in range(1, NX):
        to_row(o).wait_send()
    for o in range(1, NR):

        @pl.when(sends_to(o))
        def _():
            for i in range(3):
                to_taker(i, o).wait_send()

    @pl.when(takes)
    def _():
        for i in range(2):
            for o in range(1, NR):
                to_rows_of_span(i, o).wait_send()

    for o in range(1, NX):

        @pl.when(x + o < NX)
        def _():
            for i in range(2):
                to_owner(i, o).wait_send()

    own_out.wait()
    for o in range(1, NH):
        to_tokens(o).wait()


def shards(queries, keys, values, cache_keys, cache_values, levels, first_span, level_gate):
    hbm = pl.BlockSpec(memory_space=pl.ANY)
    smem = pl.BlockSpec(memory_space=pltpu.SMEM)
    dma = pltpu.SemaphoreType.DMA
    return pl.pallas_call(
        kernel,
        out_shape=jax.ShapeDtypeStruct((TOK, NH * WIDTH), BF),
        in_specs=[hbm, hbm, hbm, hbm, hbm, smem, smem, hbm],
        out_specs=hbm,
        scratch_shapes=[
            pltpu.VMEM((NZ, ROWS, WIDTH), BF),
            pltpu.VMEM((NZ, WIDTH, ROWS), BF),
            pltpu.VMEM((ROWS, WIDTH), BF),
            pltpu.VMEM((16, WIDTH), F32),
            pltpu.VMEM((ROWS, WIDTH), BF),
            pltpu.VMEM((ROWS, WIDTH), BF),
            pltpu.VMEM((ROWS, WIDTH), BF),
            pltpu.VMEM((NX, ROWS, WIDTH), BF),
            pltpu.VMEM((J, HD, QS), BF),
            pltpu.VMEM((J, HD, QS), F32),
            pltpu.VMEM((J, 1, QS), F32),
            pltpu.VMEM((J, 1, QS), F32),
            pltpu.VMEM((NR, ROWS, HD), BF),
            pltpu.VMEM((NR, ROWS, HD), BF),
            pltpu.VMEM((NR, ROWS, HD), BF),
            pltpu.VMEM((NR, HD, ROWS), BF),
            pltpu.VMEM((NR, 8, ROWS), F32),
            pltpu.VMEM((J, HD, ROWS), BF),
            pltpu.VMEM((J, 8, ROWS), F32),
            pltpu.VMEM((NX, WIDTH, ROWS), BF),
            pltpu.VMEM((NX, 8, ROWS), F32),
            pltpu.VMEM((NX, WIDTH, ROWS), BF),
            pltpu.VMEM((NX, 8, ROWS), F32),
            pltpu.VMEM((ROWS, WIDTH), BF),
            dma((2, 2, 9)),
            dma((2, 2, 9)),
            dma((3, NH)),
            dma((3, NH)),
            dma((NX,)),
            dma((NX,)),
            dma((3, NR)),
            dma((3, NR)),
            dma((2, NR)),
            dma((2, NR)),
            dma((2, NX)),
            dma((2, NX)),
            dma((NH,)),
            dma((NH,)),
            dma((6,)),
        ],
        compiler_params=pltpu.CompilerParams(
            collective_id=0, has_side_effects=True, vmem_limit_bytes=48 << 20
        ),
    )(queries, keys, values, cache_keys, cache_values, levels, first_span, level_gate)


def solution(mesh):
    tokens = P(("span", "head"), None)
    placed = (
        tokens, tokens, tokens, P("span", "head"), P("span", "head"), P(), P(), P(None, "head"),
    )
    return jax.shard_map(shards, mesh=mesh, in_specs=placed, out_specs=tokens, check_vma=False)
```

time: 365 us -> 78.1 us (0.21)
  the two profiles are of different devices: /device:TPU:1 before, /device:TPU:5 now
where the time goes in v1:
time: 78.1 us; the launch traced here: 77.7 us
  Pallas kernels  70.6 us (90%)
  local copies, waits for them, and re-layouts  7.15 us (9%)
    pallas_call x1, Pallas kernels, shards(): pl.pallas_call(kernel, out_shape=jax.ShapeDtypeStruct((TOK, NH * WIDTH),...  70.6 us
    unnamed x17, local copies, waits for them, and re-layouts  7.15 us

profile of v1, /device:TPU:5, one launch (start us, length us, event | category | flops | bytes accessed | tf_op | source)
XLA Modules:
  0.0 77.7 jit_solution(2714673562247186144)
XLA Ops:
  0.0 0.0 copy-start
  0.0 0.9 %copy-done = bf16[16,3072]{1,0:T(8,128)(2,1)S(1)} copy-done((bf16[16,3072]{1,0:T(8,128)(2,1)S(1)}, bf16[16,3072]{1,0:T(8,128)(2,1)}, u32[]{:S(2)}) %copy-start) | copy-done | bytes 98328
  0.9 0.0 copy-start.1
  0.9 0.9 %copy-done.1 = bf16[16,3072]{1,0:T(8,128)(2,1)S(1)} copy-done((bf16[16,3072]{1,0:T(8,128)(2,1)S(1)}, bf16[16,3072]{1,0:T(8,128)(2,1)}, u32[]{:S(2)}) %copy-start.1) | copy-done | bytes 98328
  1.8 0.0 copy-start.2
  1.8 0.9 %copy-done.2 = bf16[16,3072]{1,0:T(8,128)(2,1)S(1)} copy-done((bf16[16,3072]{1,0:T(8,128)(2,1)S(1)}, bf16[16,3072]{1,0:T(8,128)(2,1)}, u32[]{:S(2)}) %copy-start.2) | copy-done | bytes 98328
  2.7 0.0 copy-start.3
  2.7 0.9 %copy-done.3 = bf16[128,384]{1,0:T(8,128)(2,1)S(1)} copy-done((bf16[128,384]{1,0:T(8,128)(2,1)S(1)}, bf16[128,384]{1,0:T(8,128)(2,1)}, u32[]{:S(2)}) %copy-start.3) | copy-done | bytes 98328
  3.6 0.0 copy-start.4
  3.6 0.9 %copy-done.4 = bf16[128,384]{1,0:T(8,128)(2,1)S(1)} copy-done((bf16[128,384]{1,0:T(8,128)(2,1)S(1)}, bf16[128,384]{1,0:T(8,128)(2,1)}, u32[]{:S(2)}) %copy-start.4) | copy-done | bytes 98328
  4.5 0.0 copy-start.5
  4.5 0.7 copy-done.5
  5.2 0.0 copy-start.6
  5.2 0.7 copy-done.6
  5.9 0.0 copy-start.7
  5.9 0.7 copy-done.7
  6.5 70.6 %shard_map.82 = bf16[16,3072]{1,0:T(8,128)(2,1)S(1)} custom-call(bf16[16,3072]{1,0:T(8,128)(2,1)S(1)} %copy-done, bf16[16,3072]{1,0:T(8,128)(2,1)S(1)} %copy-done.1, bf16[16,3072]{1,0:T(8,128)(2,1)S(1)} %copy-done.2, bf16[128,384]{1,0:T(8,128)(2,1)S(1)} %copy-done.3, bf16[128,384]{1,0:T(8,128)(2,1)S(1)} %copy-done.4, s32[16]{0:T(128)S(1)} %copy-done.6, ...), custom_call_target="tpu_custom_call" | custom-call | tf_op jit(solution)/shard_map/pallas_call | solution.py:392
  77.1 0.6 copy.10
Async XLA Ops:
  0.0 0.9 %copy-start = (bf16[16,3072]{1,0:T(8,128)(2,1)S(1)}, bf16[16,3072]{1,0:T(8,128)(2,1)}, u32[]{:S(2)}) copy-start(bf16[16,3072]{1,0:T(8,128)(2,1)} %q_in.1) | copy-start | bytes 294916
  0.9 0.9 %copy-start.1 = (bf16[16,3072]{1,0:T(8,128)(2,1)S(1)}, bf16[16,3072]{1,0:T(8,128)(2,1)}, u32[]{:S(2)}) copy-start(bf16[16,3072]{1,0:T(8,128)(2,1)} %k_in.1) | copy-start | bytes 294916
  1.8 0.9 %copy-start.2 = (bf16[16,3072]{1,0:T(8,128)(2,1)S(1)}, bf16[16,3072]{1,0:T(8,128)(2,1)}, u32[]{:S(2)}) copy-start(bf16[16,3072]{1,0:T(8,128)(2,1)} %v_in.1) | copy-start | bytes 294916
  2.7 0.9 %copy-start.3 = (bf16[128,384]{1,0:T(8,128)(2,1)S(1)}, bf16[128,384]{1,0:T(8,128)(2,1)}, u32[]{:S(2)}) copy-start(bf16[128,384]{1,0:T(8,128)(2,1)} %ck_in.1) | copy-start | bytes 294916
  3.6 0.9 %copy-start.4 = (bf16[128,384]{1,0:T(8,128)(2,1)S(1)}, bf16[128,384]{1,0:T(8,128)(2,1)}, u32[]{:S(2)}) copy-start(bf16[128,384]{1,0:T(8,128)(2,1)} %cv_in.1) | copy-start | bytes 294916
  4.5 0.7 copy-start.5
  5.2 0.7 copy-start.6
  5.9 0.7 copy-start.7

commit v2 on v1

v2 whole, which is shorter than its diff:
```python
import functools
import math

import jax
import jax.numpy as jnp
from jax import lax
from jax.experimental import pallas as pl
from jax.experimental.pallas import tpu as pltpu
from jax.sharding import PartitionSpec as P

HD = 128
CL = 512
NX, NZ, NH = 4, 16, 8
NR = 4
J = 3
ROWS = 128
WIDTH = J * HD
TOK = 16
QS = NX * ROWS
LOW = -3.0e38
SCALE = HD**-0.5 * math.log2(math.e)
BF = jnp.bfloat16
F32 = jnp.float32
MESH = pl.DeviceIdType.MESH


def kernel(
    q_in, k_in, v_in, ck_in, cv_in, levels_in, first_in, gate_in, out,
    levels, first, kb, vt, cvv, gate, q_all, k_all, v_all, qx, qt, acc, m_st, l_st,
    cq, ck2, cv2, o_send, o_cur, p_send, p_rec, o_fin,
    ring_s, ring_r, y_s, y_r, x_s, x_r, c_s, c_r, oc_s, oc_r, p_s, p_r, out_s, out_r, loc, fetch,
):
    s = lax.axis_index("span")
    h = lax.axis_index("head")
    x = s // NZ
    z = s % NZ
    zq = z // NR
    r = z % NR
    core = h % 2

    def at(xx, zz):
        return xx * NZ + zz

    right = at(x, (z + 1) % NZ)
    left = at(x, (z + NZ - 1) % NZ)

    def remote(src, dst, send, recv, span, head):
        return pltpu.make_async_remote_copy(
            src_ref=src, dst_ref=dst, send_sem=send, recv_sem=recv,
            device_id=(span, head), device_id_type=MESH,
        )

    barrier = pltpu.get_barrier_semaphore()
    for n in (right, left):
        pl.semaphore_signal(barrier, inc=1, device_id=(n, h), device_id_type=MESH)
    for o in range(1, NR):
        pl.semaphore_signal(
            barrier, inc=1, device_id=(at(x, zq * NR + (r + o) % NR), h), device_id_type=MESH
        )
    for o in range(1, NX):
        pl.semaphore_signal(barrier, inc=1, device_id=(at((x + o) % NX, z), h), device_id_type=MESH)
    for o in range(1, NH):
        pl.semaphore_signal(barrier, inc=1, device_id=(s, (h + o) % NH), device_id_type=MESH)

    operands = (
        (cv_in, cvv), (ck_in, kb.at[0]), (gate_in, gate), (levels_in, levels), (first_in, first),
    )
    fetched = [pltpu.make_async_copy(a, b, fetch.at[i]) for i, (a, b) in enumerate(operands)]
    for copy in fetched:
        copy.start()
    fetched[0].wait()
    for j in range(J):
        vt[0, j * HD : (j + 1) * HD, :] = cvv[:, j * HD : (j + 1) * HD].T
    fetched[1].wait()

    pl.semaphore_wait(barrier, 2 + NR - 1 + NX - 1 + NH - 1)

    def ring(d, kv, c, t):
        buf, half = ((kb, ROWS // 2), (vt, WIDTH // 2))[kv]
        rows = pl.ds(c * half, half)
        if d == 0:
            src, dst, n = t - 1, t, right
        else:
            src, dst, n = (NZ + 1 - t if not isinstance(t, int) or t > 1 else 0), NZ - t, left
        return remote(
            buf.at[src, rows], buf.at[dst, rows], ring_s.at[d, kv, c, t], ring_r.at[d, kv, c, t], n, h
        )

    halves = [(kv, c) for kv in (0, 1) for c in (0, 1)]
    for kv, c in halves:
        for d in (0, 1):
            ring(d, kv, c, 1).start()

    fresh = ((q_in, q_all), (k_in, k_all), (v_in, v_all))

    def to_heads(i, o):
        src, dst = fresh[i]
        n = (h + o) % NH
        return remote(
            src.at[:, pl.ds(pl.multiple_of(n * WIDTH, HD), WIDTH)],
            dst.at[pl.ds(pl.multiple_of(h * TOK, TOK), TOK), :],
            y_s.at[i, o], y_r.at[i, o], s, n,
        )

    def own_heads(i):
        src, dst = fresh[i]
        return pltpu.make_async_copy(
            src.at[:, pl.ds(pl.multiple_of(h * WIDTH, HD), WIDTH)],
            dst.at[pl.ds(pl.multiple_of(h * TOK, TOK), TOK), :],
            loc.at[i],
        )

    for i in range(3):
        own_heads(i).start()
        for o in range(1, NH):
            to_heads(i, o).start()

    def heads_arrived(i):
        own_heads(i).wait()
        for o in range(1, NH):
            to_heads(i, o).wait_recv()

    def to_row(o):
        return remote(q_all, qx.at[x], x_s.at[o], x_r.at[o], at((x + o) % NX, z), h)

    mine = r - core
    takes = (mine >= 0) & (mine < J)

    def to_taker(i, o):
        n = (r + o) % NR
        j = jnp.clip(n - core, 0, J - 1)
        src = (q_all, k_all, v_all)[i].at[:, pl.ds(pl.multiple_of(j * HD, HD), HD)]
        dst = (cq, ck2, cv2)[i].at[r]
        return remote(src, dst, c_s.at[i, o], c_r.at[i, o], at(x, zq * NR + n), h)

    def own_taken(i):
        j = jnp.clip(mine, 0, J - 1)
        src = (q_all, k_all, v_all)[i].at[:, pl.ds(pl.multiple_of(j * HD, HD), HD)]
        return pltpu.make_async_copy(src, (cq, ck2, cv2)[i].at[r], loc.at[3 + i])

    def sends_to(o):
        n = (r + o) % NR
        return (n - core >= 0) & (n - core < J)

    def forward(t):
        for kv, c in halves:
            for d in (0, 1):
                ring(d, kv, c, t).wait_recv()
                ring(d, kv, c, t + 1).start()

    forward(1)

    heads_arrived(0)
    for o in range(1, NX):
        to_row(o).start()
    own_q = pltpu.make_async_copy(q_all, qx.at[x], loc.at[0])
    own_q.start()

    heads_arrived(1)
    heads_arrived(2)
    for o in range(1, NR):

        @pl.when(sends_to(o))
        def _():
            for i in range(3):
                to_taker(i, o).start()

    @pl.when(takes)
    def _():
        for i in range(3):
            own_taken(i).start()

    forward(2)

    acc[...] = jnp.zeros_like(acc)
    m_st[...] = jnp.full_like(m_st, LOW)
    l_st[...] = jnp.zeros_like(l_st)
    for i in range(1, NX):

        @pl.when(i > x)
        def _():
            p_rec[i] = jnp.zeros((J, HD + 16, ROWS), BF)

    for i in range(2, 5):
        fetched[i].wait()
    own_q.wait()
    for o in range(1, NX):
        to_row(o).wait_recv()
    for i in range(NX):
        for j in range(J):
            qt[j, :, i * ROWS : (i + 1) * ROWS] = qx[i, :, j * HD : (j + 1) * HD].T

    lane_row = lax.broadcasted_iota(jnp.int32, (1, QS), 1) // ROWS
    q_span = lane_row * NR + zq
    q_first = jnp.zeros((1, QS), jnp.int32)
    for i in range(NX):
        q_first = jnp.where(lane_row == i, first[i * NR + zq], q_first)

    def sees(slot):
        c = x * NR + ((z - slot + NZ) % NZ) // NR
        return (q_first <= c) & (q_span > c)

    def attend_head(j, slots):
        cols = slice(j * HD, (j + 1) * HD)
        query = qt[j]
        seen = [sees(i) for i in slots]
        scores = [jnp.dot(kb[i, :, cols], query, preferred_element_type=F32) for i in slots]
        old = m_st[j]
        peak = old
        for see, score in zip(seen, scores):
            peak = jnp.maximum(peak, jnp.where(see, jnp.max(score, axis=0, keepdims=True) * SCALE, LOW))
        shrink = jnp.exp2(old - peak)
        total = l_st[j] * shrink
        product = acc[j] * shrink
        for i, see, score in zip(slots, seen, scores):
            weight = jnp.exp2(score * SCALE - jnp.where(see, peak, jnp.inf))
            total += jnp.sum(weight, axis=0, keepdims=True)
            product += jnp.dot(vt[i, cols, :], weight.astype(BF), preferred_element_type=F32)
        m_st[j] = peak
        l_st[j] = total
        acc[j] = product

    def attend(*slots):
        for j in range(J):
            attend_head(j, slots)

    def packed(part, peak, total):
        row = lax.broadcasted_iota(jnp.int32, (16, ROWS), 0)
        tile = jnp.zeros((16, ROWS), F32)
        for first_row, value in ((0, peak), (3, total)):
            for i in range(3):
                piece = value.astype(BF).astype(F32)
                tile = jnp.where(row == first_row + i, piece, tile)
                value = value - piece
        return jnp.concatenate([part, tile], axis=0).astype(BF)

    def unpacked(block):
        tile = block[HD:].astype(F32)
        return block[:HD].astype(F32), tile[0:1] + tile[1:2] + tile[2:3], tile[3:4] + tile[4:5] + tile[5:6]

    attend(0)
    attend(1, NZ - 1)
    forward(3)
    attend(2, NZ - 2)
    forward(4)

    def to_rows_of_span(o):
        n = (r + o) % NR
        j = jnp.clip(mine, 0, J - 1)
        return remote(o_send.at[n], o_cur.at[j], oc_s.at[o], oc_r.at[o], at(x, zq * NR + n), h)

    own_part = pltpu.make_async_copy(o_send.at[r], o_cur.at[jnp.clip(mine, 0, J - 1)], loc.at[3])

    @pl.when(takes)
    def _():
        for i in range(3):
            own_taken(i).wait()
            for o in range(1, NR):
                to_taker(i, o).wait_recv()
        query = jnp.concatenate([cq[i].T for i in range(NR)], axis=1)
        keys = ck2[...].reshape(CL, HD)
        value = jnp.concatenate([cv2[i].T for i in range(NR)], axis=1)
        scores = jnp.dot(keys, query, preferred_element_type=F32)
        peak = jnp.max(scores, axis=0, keepdims=True) * SCALE
        weights = jnp.exp2(scores * SCALE - peak)
        total = jnp.sum(weights, axis=0, keepdims=True)
        part = jnp.dot(value, weights.astype(BF), preferred_element_type=F32) / total
        for i in range(NR):
            lanes = slice(i * ROWS, (i + 1) * ROWS)
            o_send[i] = packed(part[:, lanes], peak[:, lanes], total[:, lanes])
        own_part.start()
        for o in range(1, NR):
            to_rows_of_span(o).start()

    forward(5)
    attend(3, NZ - 3)
    attend(4, NZ - 4)
    forward(6)
    attend(5, NZ - 5)
    for kv, c in halves:
        for d in (0, 1):
            ring(d, kv, c, 7).wait_recv()
        ring(kv, kv, c, 8).start()
    attend(6, NZ - 6)
    attend(7, NZ - 7)

    level = levels[x * NR + zq]
    level_row = lax.broadcasted_iota(jnp.int32, (16, WIDTH), 0)
    gate_row = jnp.sum(jnp.where(level_row == level, gate[...], 0.0), axis=0, keepdims=True)

    def to_owner(j, o):
        n = (x + o) % NX
        return remote(p_send.at[n, j], p_rec.at[x, j], p_s.at[j, o], p_r.at[j, o], at(n, z), h)

    for kv, c in halves:
        ring(kv, kv, c, 8).wait_recv()
    for j in range(J):
        attend_head(j, (8,))
        for i in range(NX):
            lanes = slice(i * ROWS, (i + 1) * ROWS)
            total = l_st[j][:, lanes]
            part = acc[j][:, lanes] / jnp.where(total > 0.0, total, 1.0)
            p_send[i, j] = packed(part, m_st[j][:, lanes], total)
        for o in range(1, NX):

            @pl.when(x + o < NX)
            def _():
                to_owner(j, o).start()

    for kv, c in halves:
        for d in (0, 1):
            for t in range(1, 8):
                ring(d, kv, c, t).wait_send()
        ring(kv, kv, c, 8).wait_send()
    for i in range(3):
        for o in range(1, NH):
            to_heads(i, o).wait_send()
    for o in range(1, NX):
        to_row(o).wait_send()
    for o in range(1, NR):

        @pl.when(sends_to(o))
        def _():
            for i in range(3):
                to_taker(i, o).wait_send()

    @pl.when(takes)
    def _():
        own_part.wait()
        for o in range(1, NR):
            to_rows_of_span(o).wait_send()

    for o in range(1, NR):
        n = (r - o + NR) % NR

        @pl.when((n - core >= 0) & (n - core < J))
        def _():
            remote(
                o_send.at[0], o_cur.at[jnp.clip(n - core, 0, J - 1)], oc_s.at[o], oc_r.at[o],
                at(x, zq * NR + n), h,
            ).wait_recv()

    def to_tokens(j, o):
        n = (h + o) % NH
        return remote(
            o_fin.at[j, pl.ds(pl.multiple_of(n * TOK, TOK), TOK), :],
            out.at[:, pl.ds(pl.multiple_of(h * WIDTH + j * HD, HD), HD)],
            out_s.at[j, o], out_r.at[j, o], s, n,
        )

    def own_tokens(j):
        return pltpu.make_async_copy(
            o_fin.at[j, pl.ds(pl.multiple_of(h * TOK, TOK), TOK), :],
            out.at[:, pl.ds(pl.multiple_of(h * WIDTH + j * HD, HD), HD)],
            loc.at[j],
        )

    for j in range(J):
        for o in range(1, NX):

            @pl.when(x - o >= 0)
            def _():
                to_owner(j, o).wait_recv()

        p_rec[x, j] = p_send[x, j]
        parts = [unpacked(o_cur[j])]
        for i in range(NX):
            part, peak, total = unpacked(p_rec[i, j])
            parts.append((part, jnp.where(i <= x, peak, LOW), jnp.where(i <= x, total, 0.0)))
        peak = functools.reduce(jnp.maximum, [p for _, p, _ in parts])
        shares = [t * jnp.exp2(p - peak) for _, p, t in parts]
        whole = functools.reduce(jnp.add, shares)
        mixed = functools.reduce(jnp.add, [w * p for w, (p, _, _) in zip(shares, parts)]) / whole
        o_fin[j] = (mixed.T * gate_row[:, j * HD : (j + 1) * HD]).astype(BF)
        for o in range(1, NH):
            to_tokens(j, o).start()
        own_tokens(j).start()

    for j in range(J):
        for o in range(1, NX):

            @pl.when(x + o < NX)
            def _():
                to_owner(j, o).wait_send()

        own_tokens(j).wait()
        for o in range(1, NH):
            to_tokens(j, o).wait()


def shards(queries, keys, values, cache_keys, cache_values, levels, first_span, level_gate):
    hbm = pl.BlockSpec(memory_space=pltpu.HBM)
    dma = pltpu.SemaphoreType.DMA
    return pl.pallas_call(
        kernel,
        out_shape=pltpu.VMEM((TOK, NH * WIDTH), BF),
        in_specs=[hbm] * 8,
        out_specs=pl.BlockSpec(memory_space=pltpu.VMEM),
        scratch_shapes=[
            pltpu.SMEM((16,), jnp.int32),
            pltpu.SMEM((16,), jnp.int32),
            pltpu.VMEM((NZ, ROWS, WIDTH), BF),
            pltpu.VMEM((NZ, WIDTH, ROWS), BF),
            pltpu.VMEM((ROWS, WIDTH), BF),
            pltpu.VMEM((16, WIDTH), F32),
            pltpu.VMEM((ROWS, WIDTH), BF),
            pltpu.VMEM((ROWS, WIDTH), BF),
            pltpu.VMEM((ROWS, WIDTH), BF),
            pltpu.VMEM((NX, ROWS, WIDTH), BF),
            pltpu.VMEM((J, HD, QS), BF),
            pltpu.VMEM((J, HD, QS), F32),
            pltpu.VMEM((J, 1, QS), F32),
            pltpu.VMEM((J, 1, QS), F32),
            pltpu.VMEM((NR, ROWS, HD), BF),
            pltpu.VMEM((NR, ROWS, HD), BF),
            pltpu.VMEM((NR, ROWS, HD), BF),
            pltpu.VMEM((NR, HD + 16, ROWS), BF),
            pltpu.VMEM((J, HD + 16, ROWS), BF),
            pltpu.VMEM((NX, J, HD + 16, ROWS), BF),
            pltpu.VMEM((NX, J, HD + 16, ROWS), BF),
            pltpu.VMEM((J, ROWS, HD), BF),
            dma((2, 2, 2, 9)),
            dma((2, 2, 2, 9)),
            dma((3, NH)),
            dma((3, NH)),
            dma((NX,)),
            dma((NX,)),
            dma((3, NR)),
            dma((3, NR)),
            dma((NR,)),
            dma((NR,)),
            dma((J, NX)),
            dma((J, NX)),
            dma((J, NH)),
            dma((J, NH)),
            dma((6,)),
            dma((5,)),
        ],
        compiler_params=pltpu.CompilerParams(
            collective_id=0, has_side_effects=True, vmem_limit_bytes=63 << 20
        ),
    )(queries, keys, values, cache_keys, cache_values, levels, first_span, level_gate)


def solution(mesh):
    tokens = P(("span", "head"), None)
    placed = (
        tokens, tokens, tokens, P("span", "head"), P("span", "head"), P(), P(), P(None, "head"),
    )
    return jax.shard_map(shards, mesh=mesh, in_specs=placed, out_specs=tokens, check_vma=False)
```

time: 78.1 us -> 67.2 us (0.86)
  local copies, waits for them, and re-layouts: 7.15 us -> 0.64 us
  Pallas kernels: 70.6 us -> 66.4 us
    unnamed x17 -> x1, local copies, waits for them, and re-layouts: 7.15 us -> 0.64 us
    pallas_call x1, Pallas kernels: 70.6 us -> 66.4 us  [shards(): pl.pallas_call(kernel, out_shape=pltpu.VMEM((TOK, NH * WIDTH), BF), in_sp...]
where the time goes in v2:
time: 67.2 us; the launch traced here: 67.1 us
  Pallas kernels  66.4 us (99%)
    pallas_call x1, Pallas kernels, shards(): pl.pallas_call(kernel, out_shape=pltpu.VMEM((TOK, NH * WIDTH), BF), in_sp...  66.4 us

profile of v2, /device:TPU:5, one launch (start us, length us, event | category | flops | bytes accessed | tf_op | source)
XLA Modules:
  0.0 67.1 jit_solution(6563158123823882473)
XLA Ops:
  0.0 66.4 %shard_map.82 = bf16[16,3072]{1,0:T(8,128)(2,1)S(1)} custom-call(bf16[16,3072]{1,0:T(8,128)(2,1)} %q_in.1, bf16[16,3072]{1,0:T(8,128)(2,1)} %k_in.1, bf16[16,3072]{1,0:T(8,128)(2,1)} %v_in.1, bf16[128,384]{1,0:T(8,128)(2,1)} %ck_in.1, bf16[128,384]{1,0:T(8,128)(2,1)} %cv_in.1, s32[16]{0:T(128)} %levels_in.1, s32[16]{0:T(128)} %first_in.1, f32[16,384]{1,0:T(8,128)} %gate_in.1), custom_call_target="tpu_custom_call" | custom-call | tf_op jit(solution)/shard_map/pallas_call | solution.py:394
  66.4 0.6 copy.10

commit v3 on v2

v3 whole, which is shorter than its diff:
```python
import functools
import math

import jax
import jax.numpy as jnp
from jax import lax
from jax.experimental import pallas as pl
from jax.experimental.pallas import tpu as pltpu
from jax.sharding import PartitionSpec as P

HD = 128
CL = 512
NX, NZ, NH = 4, 16, 8
NR = 4
J = 3
ROWS = 128
WIDTH = J * HD
TOK = 16
QS = NX * ROWS
LOW = -3.0e38
SCALE = HD**-0.5 * math.log2(math.e)
BF = jnp.bfloat16
F32 = jnp.float32
MESH = pl.DeviceIdType.MESH


def kernel(
    q_in, k_in, v_in, ck_in, cv_in, levels_in, first_in, gate_in, out,
    levels, first, kb, vt, cvv, gate, q_all, k_all, v_all, qx, qt, acc, m_st, l_st,
    cq, ck2, cv2, o_send, o_cur, p_send, p_rec, gate_cols,
    ring_s, ring_r, y_s, y_r, x_s, x_r, c_s, c_r, oc_s, oc_r, p_s, p_r, loc, fetch,
):
    s = lax.axis_index("span")
    h = lax.axis_index("head")
    x = s // NZ
    z = s % NZ
    zq = z // NR
    r = z % NR
    core = h % 2

    def at(xx, zz):
        return xx * NZ + zz

    right = at(x, (z + 1) % NZ)
    left = at(x, (z + NZ - 1) % NZ)

    def remote(src, dst, send, recv, span, head):
        return pltpu.make_async_remote_copy(
            src_ref=src, dst_ref=dst, send_sem=send, recv_sem=recv,
            device_id=(span, head), device_id_type=MESH,
        )

    barrier = pltpu.get_barrier_semaphore()
    for n in (right, left):
        pl.semaphore_signal(barrier, inc=1, device_id=(n, h), device_id_type=MESH)
    for o in range(1, NR):
        pl.semaphore_signal(
            barrier, inc=1, device_id=(at(x, zq * NR + (r + o) % NR), h), device_id_type=MESH
        )
    for o in range(1, NX):
        pl.semaphore_signal(barrier, inc=1, device_id=(at((x + o) % NX, z), h), device_id_type=MESH)
    for o in range(1, NH):
        pl.semaphore_signal(barrier, inc=1, device_id=(s, (h + o) % NH), device_id_type=MESH)

    operands = (
        (cv_in, cvv), (ck_in, kb.at[0]), (gate_in, gate), (levels_in, levels), (first_in, first),
    )
    fetched = [pltpu.make_async_copy(a, b, fetch.at[i]) for i, (a, b) in enumerate(operands)]
    for copy in fetched:
        copy.start()
    pl.semaphore_wait(barrier, 2 + NR - 1 + NX - 1 + NH - 1)

    def ring(d, kv, c, t):
        buf, half = ((kb, ROWS // 2), (vt, WIDTH // 2))[kv]
        rows = pl.ds(c * half, half)
        if d == 0:
            src, dst, n = t - 1, t, right
        else:
            src, dst, n = (NZ + 1 - t) % NZ, NZ - t, left
        source = ck_in.at[rows] if t == 1 and kv == 0 else buf.at[src, rows]
        return remote(source, buf.at[dst, rows], ring_s.at[d, kv, c, t], ring_r.at[d, kv, c, t], n, h)

    halves = [(kv, c) for kv in (0, 1) for c in (0, 1)]
    fresh = ((q_in, q_all), (k_in, k_all), (v_in, v_all))

    def to_heads(i, o):
        src, dst = fresh[i]
        n = (h + o) % NH
        return remote(
            src.at[:, pl.ds(pl.multiple_of(n * WIDTH, HD), WIDTH)],
            dst.at[pl.ds(pl.multiple_of(h * TOK, TOK), TOK), :],
            y_s.at[i, o], y_r.at[i, o], s, n,
        )

    def own_heads(i):
        src, dst = fresh[i]
        return pltpu.make_async_copy(
            src.at[:, pl.ds(pl.multiple_of(h * WIDTH, HD), WIDTH)],
            dst.at[pl.ds(pl.multiple_of(h * TOK, TOK), TOK), :],
            loc.at[i],
        )

    def send_heads(i):
        own_heads(i).start()
        for o in range(1, NH):
            to_heads(i, o).start()

    send_heads(0)
    for c in (0, 1):
        for d in (0, 1):
            ring(d, 0, c, 1).start()
    fetched[0].wait()
    for j in range(J):
        vt[0, j * HD : (j + 1) * HD, :] = cvv[:, j * HD : (j + 1) * HD].T
    for c in (0, 1):
        for d in (0, 1):
            ring(d, 1, c, 1).start()
    send_heads(1)
    send_heads(2)

    def heads_arrived(i):
        own_heads(i).wait()
        for o in range(1, NH):
            to_heads(i, o).wait_recv()

    def to_row(o):
        return remote(q_all, qx.at[x], x_s.at[o], x_r.at[o], at((x + o) % NX, z), h)

    mine = r - core
    takes = (mine >= 0) & (mine < J)

    def to_taker(i, o):
        n = (r + o) % NR
        j = jnp.clip(n - core, 0, J - 1)
        src = (q_all, k_all, v_all)[i].at[:, pl.ds(pl.multiple_of(j * HD, HD), HD)]
        dst = (cq, ck2, cv2)[i].at[r]
        return remote(src, dst, c_s.at[i, o], c_r.at[i, o], at(x, zq * NR + n), h)

    def own_taken(i):
        j = jnp.clip(mine, 0, J - 1)
        src = (q_all, k_all, v_all)[i].at[:, pl.ds(pl.multiple_of(j * HD, HD), HD)]
        return pltpu.make_async_copy(src, (cq, ck2, cv2)[i].at[r], loc.at[3 + i])

    def sends_to(o):
        n = (r + o) % NR
        return (n - core >= 0) & (n - core < J)

    def forward(t, *work):
        for n, (kv, c) in enumerate(halves):
            for d in (0, 1):
                ring(d, kv, c, t).wait_recv()
                if t < 7:
                    ring(d, kv, c, t + 1).start()
            if t == 7:
                last(kv, c, "start")
            for item in work[n : n + 1]:
                item()

    def sent(t):
        for kv, c in halves:
            for d in (0, 1):
                ring(d, kv, c, t).wait_send()

    def last(kv, c, what):
        getattr(ring(kv, kv, c, 8), what)()

    own_q = pltpu.make_async_copy(q_all, qx.at[x], loc.at[0])

    def share_queries():
        heads_arrived(0)
        for o in range(1, NX):
            to_row(o).start()
        own_q.start()

    def share_current():
        heads_arrived(2)
        for o in range(1, NR):

            @pl.when(sends_to(o))
            def _():
                for i in range(3):
                    to_taker(i, o).start()

        @pl.when(takes)
        def _():
            for i in range(3):
                own_taken(i).start()

    def clear():
        acc[...] = jnp.zeros_like(acc)
        m_st[...] = jnp.full_like(m_st, LOW)
        l_st[...] = jnp.zeros_like(l_st)
        for i in range(1, NX):

            @pl.when(i > x)
            def _():
                p_rec[i] = jnp.zeros((NH, TOK, WIDTH + HD), BF)

    forward(1)
    share_queries()
    heads_arrived(1)
    share_current()
    clear()

    def spread_gate(i):
        if i == 0:
            for n in range(2, 5):
                fetched[n].wait()
        level_row = lax.broadcasted_iota(jnp.int32, (16, WIDTH), 0)
        gate_row = jnp.sum(
            jnp.where(level_row == levels[i * NR + zq], gate[...], 0.0), axis=0, keepdims=True
        )
        for j in range(J):
            gate_cols[i, j] = jnp.broadcast_to(gate_row[:, j * HD : (j + 1) * HD], (ROWS, HD)).T

    forward(2, *[functools.partial(spread_gate, i) for i in range(NX)])

    fetched[1].wait()

    def turn_queries(j):
        if j == 0:
            own_q.wait()
            for o in range(1, NX):
                to_row(o).wait_recv()
        for i in range(NX):
            qt[j, :, i * ROWS : (i + 1) * ROWS] = qx[i, :, j * HD : (j + 1) * HD].T

    forward(3, *[functools.partial(turn_queries, j) for j in range(J)])

    lane_row = lax.broadcasted_iota(jnp.int32, (1, QS), 1) // ROWS
    q_span = lane_row * NR + zq
    q_first = jnp.zeros((1, QS), jnp.int32)
    for i in range(NX):
        q_first = jnp.where(lane_row == i, first[i * NR + zq], q_first)

    def sees(slot):
        c = x * NR + ((z - slot + NZ) % NZ) // NR
        return (q_first <= c) & (q_span > c)

    def attend_head(j, slots):
        cols = slice(j * HD, (j + 1) * HD)
        query = qt[j]
        seen = [sees(i) for i in slots]
        scores = [jnp.dot(kb[i, :, cols], query, preferred_element_type=F32) for i in slots]
        old = m_st[j]
        peak = old
        for see, score in zip(seen, scores):
            peak = jnp.maximum(peak, jnp.where(see, jnp.max(score, axis=0, keepdims=True) * SCALE, LOW))
        shrink = jnp.exp2(old - peak)
        total = l_st[j] * shrink
        product = acc[j] * shrink
        for i, see, score in zip(slots, seen, scores):
            weight = jnp.exp2(score * SCALE - jnp.where(see, peak, jnp.inf))
            total += jnp.sum(weight, axis=0, keepdims=True)
            product += jnp.dot(vt[i, cols, :], weight.astype(BF), preferred_element_type=F32)
        m_st[j] = peak
        l_st[j] = total
        acc[j] = product

    def head(j, *slots):
        return functools.partial(attend_head, j, slots)

    def both(*items):
        def run():
            for item in items:
                item()

        return run

    def packed(part, peak, total):
        row = lax.broadcasted_iota(jnp.int32, (16, ROWS), 0)
        tile = jnp.zeros((16, ROWS), F32)
        for first_row, value in ((0, peak), (3, total)):
            for i in range(3):
                piece = value.astype(BF).astype(F32)
                tile = jnp.where(row == first_row + i, piece, tile)
                value = value - piece
        return jnp.concatenate([part, tile], axis=0).astype(BF)

    def unpacked(block):
        tile = block[HD:].astype(F32)
        return block[:HD].astype(F32), tile[0:1] + tile[1:2] + tile[2:3], tile[3:4] + tile[4:5] + tile[5:6]

    def to_rows_of_span(o):
        n = (r + o) % NR
        j = jnp.clip(mine, 0, J - 1)
        return remote(o_send.at[n], o_cur.at[j], oc_s.at[o], oc_r.at[o], at(x, zq * NR + n), h)

    own_part = pltpu.make_async_copy(o_send.at[r], o_cur.at[jnp.clip(mine, 0, J - 1)], loc.at[3])

    def current(n):
        @pl.when(takes)
        def _():
            if n == 0:
                for i in range(3):
                    own_taken(i).wait()
                    for o in range(1, NR):
                        to_taker(i, o).wait_recv()
            keys = ck2[...].reshape(CL, HD)
            scores = jnp.dot(keys, cq[n].T, preferred_element_type=F32)
            peak = jnp.max(scores, axis=0, keepdims=True) * SCALE
            weights = jnp.exp2(scores * SCALE - peak)
            total = jnp.sum(weights, axis=0, keepdims=True)
            value = jnp.concatenate([cv2[i].T for i in range(NR)], axis=1)
            part = jnp.dot(value, weights.astype(BF), preferred_element_type=F32) * (1.0 / total)
            o_send[n] = packed(part, peak, total)
            if n == NR - 1:
                own_part.start()
                for o in range(1, NR):
                    to_rows_of_span(o).start()

    def current_arrived():
        @pl.when(takes)
        def _():
            own_part.wait()

        for o in range(1, NR):
            n = (r - o + NR) % NR

            @pl.when((n - core >= 0) & (n - core < J))
            def _():
                remote(
                    o_send.at[0], o_cur.at[jnp.clip(n - core, 0, J - 1)], oc_s.at[o], oc_r.at[o],
                    at(x, zq * NR + n), h,
                ).wait_recv()

    def merge_current(j):
        part, peak, total = unpacked(o_cur[j])
        lanes = pl.ds(pl.multiple_of(x * ROWS, ROWS), ROWS)
        old = m_st[j, :, lanes]
        new = jnp.maximum(old, peak)
        shrink, share = jnp.exp2(old - new), total * jnp.exp2(peak - new)
        m_st[j, :, lanes] = new
        l_st[j, :, lanes] = l_st[j, :, lanes] * shrink + share
        acc[j, :, lanes] = acc[j, :, lanes] * shrink + part * share

    def sent_entry():
        for i in range(3):
            for o in range(1, NH):
                to_heads(i, o).wait_send()
        for o in range(1, NX):
            to_row(o).wait_send()

    def sent_current():
        for o in range(1, NR):

            @pl.when(sends_to(o))
            def _():
                for i in range(3):
                    to_taker(i, o).wait_send()

        @pl.when(takes)
        def _():
            for o in range(1, NR):
                to_rows_of_span(o).wait_send()

    cur = [functools.partial(current, n) for n in range(NR)]
    merge = [functools.partial(merge_current, j) for j in range(J)]
    sent(1)
    forward(4, head(0, 0, 1, 15), head(1, 0, 1, 15), head(2, 0, 1, 15), cur[0])
    sent(2)
    forward(5, cur[1], cur[2], cur[3], both(head(0, 2, 14), sent_entry))
    sent(3)
    forward(
        6,
        both(head(1, 2, 14), head(2, 2, 14)), both(head(0, 3, 13), head(1, 3, 13)),
        both(head(2, 3, 13), head(0, 4, 12)), both(head(1, 4, 12), head(2, 4, 12)),
    )
    sent(4)
    forward(
        7,
        both(head(0, 5, 11), head(1, 5, 11)), both(head(2, 5, 11), current_arrived, sent_current),
        both(head(0, 6, 10), head(1, 6, 10)), both(head(2, 6, 10), *merge),
    )
    for j in range(J):
        attend_head(j, (7, 9))
    sent(5)
    sent(6)

    def to_owner(i, n):
        return remote(
            p_send.at[i, pl.ds(pl.multiple_of(n * TOK, TOK), TOK), :], p_rec.at[x, h],
            p_s.at[i, n], p_r.at[x, h], at(i, z), n,
        )

    def from_part(i, n):
        return remote(p_send.at[i, pl.ds(0, TOK), :], p_rec.at[i, n], p_s.at[i, n], p_r.at[i, n], at(i, z), n)

    own_tokens = pltpu.make_async_copy(
        p_send.at[x, pl.ds(pl.multiple_of(h * TOK, TOK), TOK), :], p_rec.at[x, h], loc.at[0]
    )

    def logs(i):
        lanes = slice(i * ROWS, (i + 1) * ROWS)
        row = lax.broadcasted_iota(jnp.int32, (ROWS, ROWS), 0)
        tile = jnp.zeros((ROWS, ROWS), F32)
        for j in range(J):
            total = l_st[j][:, lanes]
            value = jnp.where(
                total > 0.0,
                m_st[j][:, lanes] + jnp.log(jnp.where(total > 0.0, total, 1.0)) * math.log2(math.e),
                LOW,
            )
            for n in range(3):
                piece = value.astype(BF).astype(F32)
                tile = jnp.where(row == 3 * n + j, piece, tile)
                value = value - piece
        return tile.T

    for kv, c in halves:
        last(kv, c, "wait_recv")
    for j in range(J):
        attend_head(j, (8,))
    for i in reversed(range(NX)):

        @pl.when(i >= x)
        def _():
            lanes = slice(i * ROWS, (i + 1) * ROWS)
            for j in range(J):
                total = l_st[j][:, lanes]
                part = acc[j][:, lanes] * (1.0 / jnp.where(total > 0.0, total, 1.0)) * gate_cols[i, j]
                p_send[i, :, j * HD : (j + 1) * HD] = part.astype(BF).T
            p_send[i, :, WIDTH:] = logs(i).astype(BF)
            for o in range(1, NH):
                to_owner(i, (h + o) % NH).start()

            @pl.when(i > x)
            def _():
                to_owner(i, h).start()

            @pl.when(i == x)
            def _():
                own_tokens.start()

    sent(7)
    for kv, c in halves:
        last(kv, c, "wait_send")
    own_tokens.wait()
    for n in range(NH):
        for i in range(NX):

            @pl.when((i < x) | ((i == x) & (n != h)))
            def _():
                from_part(i, n).wait_recv()

        marks = []
        for i in range(NX):
            tile = p_rec[i, n, :, WIDTH:].astype(F32)
            mark = tile + pltpu.roll(tile, ROWS - 3, 1) + pltpu.roll(tile, ROWS - 6, 1)
            marks.append(jnp.where(i <= x, mark, LOW))
        peak = functools.reduce(jnp.maximum, marks)
        shares = [jnp.exp2(m - peak) for m in marks]
        scale = 1.0 / functools.reduce(jnp.add, shares)
        shares = [w * scale for w in shares]
        for j in range(J):
            cols = slice(j * HD, (j + 1) * HD)
            mixed = functools.reduce(
                jnp.add, [w[:, j : j + 1] * p_rec[i, n, :, cols].astype(F32) for i, w in enumerate(shares)]
            )
            out[:, n * WIDTH + j * HD : n * WIDTH + (j + 1) * HD] = mixed.astype(BF)

    for i in range(NX):
        for n in range(NH):

            @pl.when((i > x) | ((i == x) & (n != h)))
            def _():
                to_owner(i, n).wait_send()


def shards(queries, keys, values, cache_keys, cache_values, levels, first_span, level_gate):
    hbm = pl.BlockSpec(memory_space=pltpu.HBM)
    dma = pltpu.SemaphoreType.DMA
    return pl.pallas_call(
        kernel,
        out_shape=pltpu.VMEM((TOK, NH * WIDTH), BF),
        in_specs=[hbm] * 8,
        out_specs=pl.BlockSpec(memory_space=pltpu.VMEM),
        scratch_shapes=[
            pltpu.SMEM((16,), jnp.int32),
            pltpu.SMEM((16,), jnp.int32),
            pltpu.VMEM((NZ, ROWS, WIDTH), BF),
            pltpu.VMEM((NZ, WIDTH, ROWS), BF),
            pltpu.VMEM((ROWS, WIDTH), BF),
            pltpu.VMEM((16, WIDTH), F32),
            pltpu.VMEM((ROWS, WIDTH), BF),
            pltpu.VMEM((ROWS, WIDTH), BF),
            pltpu.VMEM((ROWS, WIDTH), BF),
            pltpu.VMEM((NX, ROWS, WIDTH), BF),
            pltpu.VMEM((J, HD, QS), BF),
            pltpu.VMEM((J, HD, QS), F32),
            pltpu.VMEM((J, 1, QS), F32),
            pltpu.VMEM((J, 1, QS), F32),
            pltpu.VMEM((NR, ROWS, HD), BF),
            pltpu.VMEM((NR, ROWS, HD), BF),
            pltpu.VMEM((NR, ROWS, HD), BF),
            pltpu.VMEM((NR, HD + 16, ROWS), BF),
            pltpu.VMEM((J, HD + 16, ROWS), BF),
            pltpu.VMEM((NX, ROWS, WIDTH + HD), BF),
            pltpu.VMEM((NX, NH, TOK, WIDTH + HD), BF),
            pltpu.VMEM((NX, J, HD, ROWS), F32),
            dma((2, 2, 2, 9)),
            dma((2, 2, 2, 9)),
            dma((3, NH)),
            dma((3, NH)),
            dma((NX,)),
            dma((NX,)),
            dma((3, NR)),
            dma((3, NR)),
            dma((NR,)),
            dma((NR,)),
            dma((NX, NH)),
            dma((NX, NH)),
            dma((6,)),
            dma((5,)),
        ],
        compiler_params=pltpu.CompilerParams(
            collective_id=0, has_side_effects=True, vmem_limit_bytes=63 << 20
        ),
    )(queries, keys, values, cache_keys, cache_values, levels, first_span, level_gate)


def solution(mesh):
    tokens = P(("span", "head"), None)
    placed = (
        tokens, tokens, tokens, P("span", "head"), P("span", "head"), P(), P(), P(None, "head"),
    )
    return jax.shard_map(shards, mesh=mesh, in_specs=placed, out_specs=tokens, check_vma=False)
```

time: 67.2 us -> 66.1 us (0.984)
  the two profiles are of different devices: /device:TPU:5 before, /device:TPU:1 now
where the time goes in v3:
time: 66.1 us; the launch traced here: 65.6 us
  Pallas kernels  65 us (98%)
    pallas_call x1, Pallas kernels, shards(): pl.pallas_call(kernel, out_shape=pltpu.VMEM((TOK, NH * WIDTH), BF), in_sp...  65 us

profile of v3, /device:TPU:1, one launch (start us, length us, event | category | flops | bytes accessed | tf_op | source)
XLA Modules:
  0.0 65.6 jit_solution(9088750080902030039)
XLA Ops:
  0.0 65.0 %shard_map.82 = bf16[16,3072]{1,0:T(8,128)(2,1)S(1)} custom-call(bf16[16,3072]{1,0:T(8,128)(2,1)} %q_in.1, bf16[16,3072]{1,0:T(8,128)(2,1)} %k_in.1, bf16[16,3072]{1,0:T(8,128)(2,1)} %v_in.1, bf16[128,384]{1,0:T(8,128)(2,1)} %ck_in.1, bf16[128,384]{1,0:T(8,128)(2,1)} %cv_in.1, s32[16]{0:T(128)} %levels_in.1, s32[16]{0:T(128)} %first_in.1, f32[16,384]{1,0:T(8,128)} %gate_in.1), custom_call_target="tpu_custom_call" | custom-call | tf_op jit(solution)/shard_map/pallas_call | solution.py:473
  65.0 0.6 copy.10

commit v4 on v3

--- a/solution.py
+++ b/solution.py
@@ -62,12 +62,8 @@
     for o in range(1, NH):
         pl.semaphore_signal(barrier, inc=1, device_id=(s, (h + o) % NH), device_id_type=MESH)
 
-    operands = (
-        (cv_in, cvv), (ck_in, kb.at[0]), (gate_in, gate), (levels_in, levels), (first_in, first),
-    )
-    fetched = [pltpu.make_async_copy(a, b, fetch.at[i]) for i, (a, b) in enumerate(operands)]
-    for copy in fetched:
-        copy.start()
+    fetch_v = pltpu.make_async_copy(cv_in, cvv, fetch.at[0])
+    fetch_v.start()
     pl.semaphore_wait(barrier, 2 + NR - 1 + NX - 1 + NH - 1)
 
     def ring(d, kv, c, t):
@@ -100,15 +96,22 @@
             loc.at[i],
         )
 
+    operands = (
+        (cv_in, cvv), (ck_in, kb.at[0]), (gate_in, gate), (levels_in, levels), (first_in, first),
+    )
+    fetched = [pltpu.make_async_copy(a, b, fetch.at[i]) for i, (a, b) in enumerate(operands)]
+
     def send_heads(i):
         own_heads(i).start()
         for o in range(1, NH):
             to_heads(i, o).start()
 
-    send_heads(0)
     for c in (0, 1):
         for d in (0, 1):
             ring(d, 0, c, 1).start()
+    for copy in fetched[1:]:
+        copy.start()
+    send_heads(0)
     fetched[0].wait()
     for j in range(J):
         vt[0, j * HD : (j + 1) * HD, :] = cvv[:, j * HD : (j + 1) * HD].T
@@ -237,25 +240,25 @@
         c = x * NR + ((z - slot + NZ) % NZ) // NR
         return (q_first <= c) & (q_span > c)
 
-    def attend_head(j, slots):
+    def attend_head(j, slots, lanes=slice(0, QS)):
         cols = slice(j * HD, (j + 1) * HD)
-        query = qt[j]
-        seen = [sees(i) for i in slots]
+        query = qt[j, :, lanes]
+        seen = [sees(i)[:, lanes] for i in slots]
         scores = [jnp.dot(kb[i, :, cols], query, preferred_element_type=F32) for i in slots]
-        old = m_st[j]
+        old = m_st[j, :, lanes]
         peak = old
         for see, score in zip(seen, scores):
             peak = jnp.maximum(peak, jnp.where(see, jnp.max(score, axis=0, keepdims=True) * SCALE, LOW))
         shrink = jnp.exp2(old - peak)
-        total = l_st[j] * shrink
-        product = acc[j] * shrink
+        total = l_st[j, :, lanes] * shrink
+        product = acc[j, :, lanes] * shrink
         for i, see, score in zip(slots, seen, scores):
             weight = jnp.exp2(score * SCALE - jnp.where(see, peak, jnp.inf))
             total += jnp.sum(weight, axis=0, keepdims=True)
             product += jnp.dot(vt[i, cols, :], weight.astype(BF), preferred_element_type=F32)
-        m_st[j] = peak
-        l_st[j] = total
-        acc[j] = product
+        m_st[j, :, lanes] = peak
+        l_st[j, :, lanes] = total
+        acc[j, :, lanes] = product
 
     def head(j, *slots):
         return functools.partial(attend_head, j, slots)
@@ -409,32 +412,41 @@
 
     for kv, c in halves:
         last(kv, c, "wait_recv")
-    for j in range(J):
-        attend_head(j, (8,))
-    for i in reversed(range(NX)):
-
-        @pl.when(i >= x)
+    def finish(i):
+        lanes = slice(i * ROWS, (i + 1) * ROWS)
+        for j in range(J):
+            attend_head(j, (8,), lanes)
+            total = l_st[j][:, lanes]
+            part = acc[j][:, lanes] * (1.0 / jnp.where(total > 0.0, total, 1.0)) * gate_cols[i, j]
+            p_send[i, :, j * HD : (j + 1) * HD] = part.astype(BF).T
+        p_send[i, :, WIDTH:] = logs(i).astype(BF)
+        for o in range(1, NH):
+            to_owner(i, (h + o) % NH).start()
+
+    for i in (1, 3, 2):
+
+        @pl.when(i > x)
         def _():
-            lanes = slice(i * ROWS, (i + 1) * ROWS)
-            for j in range(J):
-                total = l_st[j][:, lanes]
-                part = acc[j][:, lanes] * (1.0 / jnp.where(total > 0.0, total, 1.0)) * gate_cols[i, j]
-                p_send[i, :, j * HD : (j + 1) * HD] = part.astype(BF).T
-            p_send[i, :, WIDTH:] = logs(i).astype(BF)
-            for o in range(1, NH):
-                to_owner(i, (h + o) % NH).start()
-
-            @pl.when(i > x)
-            def _():
-                to_owner(i, h).start()
-
-            @pl.when(i == x)
-            def _():
-                own_tokens.start()
+            finish(i)
+            to_owner(i, h).start()
+
+    for i in range(NX):
+
+        @pl.when(i == x)
+        def _():
+            finish(i)
+            own_tokens.start()
 
     sent(7)
     for kv, c in halves:
         last(kv, c, "wait_send")
+    for i in range(NX):
+        for n in range(NH):
+
+            @pl.when((i > x) | ((i == x) & (n != h)))
+            def _():
+                to_owner(i, n).wait_send()
+
     own_tokens.wait()
     for n in range(NH):
         for i in range(NX):
@@ -458,13 +470,6 @@
                 jnp.add, [w[:, j : j + 1] * p_rec[i, n, :, cols].astype(F32) for i, w in enumerate(shares)]
             )
             out[:, n * WIDTH + j * HD : n * WIDTH + (j + 1) * HD] = mixed.astype(BF)
-
-    for i in range(NX):
-        for n in range(NH):
-
-            @pl.when((i > x) | ((i == x) & (n != h)))
-            def _():
-                to_owner(i, n).wait_send()
 
 
 def shards(queries, keys, values, cache_keys, cache_values, levels, first_span, level_gate):

time: 66.1 us -> 65.8 us (level)
  no operation moved by 1% of the time
where the time goes in v4:
time: 65.8 us; the launch traced here: 65.7 us
  Pallas kernels  65 us (99%)
    pallas_call x1, Pallas kernels, shards(): pl.pallas_call(kernel, out_shape=pltpu.VMEM((TOK, NH * WIDTH), BF), in_sp...  65 us

profile of v4, /device:TPU:1, one launch (start us, length us, event | category | flops | bytes accessed | tf_op | source)
XLA Modules:
  0.0 65.7 jit_solution(6549803900583149495)
XLA Ops:
  0.0 65.0 %shard_map.82 = bf16[16,3072]{1,0:T(8,128)(2,1)S(1)} custom-call(bf16[16,3072]{1,0:T(8,128)(2,1)} %q_in.1, bf16[16,3072]{1,0:T(8,128)(2,1)} %k_in.1, bf16[16,3072]{1,0:T(8,128)(2,1)} %v_in.1, bf16[128,384]{1,0:T(8,128)(2,1)} %ck_in.1, bf16[128,384]{1,0:T(8,128)(2,1)} %cv_in.1, s32[16]{0:T(128)} %levels_in.1, s32[16]{0:T(128)} %first_in.1, f32[16,384]{1,0:T(8,128)} %gate_in.1), custom_call_target="tpu_custom_call" | custom-call | tf_op jit(solution)/shard_map/pallas_call | solution.py:478
  65.0 0.6 copy.10

commit v5 on v4

--- a/solution.py
+++ b/solution.py
@@ -253,7 +253,7 @@
         total = l_st[j, :, lanes] * shrink
         product = acc[j, :, lanes] * shrink
         for i, see, score in zip(slots, seen, scores):
-            weight = jnp.exp2(score * SCALE - jnp.where(see, peak, jnp.inf))
+            weight = jnp.exp2(jnp.where(see, score * SCALE - peak, -jnp.inf))
             total += jnp.sum(weight, axis=0, keepdims=True)
             product += jnp.dot(vt[i, cols, :], weight.astype(BF), preferred_element_type=F32)
         m_st[j, :, lanes] = peak

time: 65.8 us -> 65.8 us (level)
  no operation moved by 1% of the time
where the time goes in v5:
time: 65.8 us; the launch traced here: 65.7 us
  Pallas kernels  65.1 us (99%)
    pallas_call x1, Pallas kernels, shards(): pl.pallas_call(kernel, out_shape=pltpu.VMEM((TOK, NH * WIDTH), BF), in_sp...  65.1 us

profile of v5, /device:TPU:1, one launch (start us, length us, event | category | flops | bytes accessed | tf_op | source)
XLA Modules:
  0.0 65.7 jit_solution(6652304160908618360)
XLA Ops:
  0.0 65.1 %shard_map.82 = bf16[16,3072]{1,0:T(8,128)(2,1)S(1)} custom-call(bf16[16,3072]{1,0:T(8,128)(2,1)} %q_in.1, bf16[16,3072]{1,0:T(8,128)(2,1)} %k_in.1, bf16[16,3072]{1,0:T(8,128)(2,1)} %v_in.1, bf16[128,384]{1,0:T(8,128)(2,1)} %ck_in.1, bf16[128,384]{1,0:T(8,128)(2,1)} %cv_in.1, s32[16]{0:T(128)} %levels_in.1, s32[16]{0:T(128)} %first_in.1, f32[16,384]{1,0:T(8,128)} %gate_in.1), custom_call_target="tpu_custom_call" | custom-call | tf_op jit(solution)/shard_map/pallas_call | solution.py:478
  65.1 0.6 copy.10
